TPU v7x, 32 devices: a whole 2x2x4 slice. The times are simulated.
32 devices in a mesh: rep: 2 (over core), fsdp: 16 (over z, y, x).
Axes of the slice: x: 2, y: 2, z: 4, core: 2. Of those that a mesh axis runs over, the one named last changes fastest.
Arguments:
- tokens: bfloat16 [4096, 8192], P('fsdp'), as said below
- query_ckpt: float32 [2, 8192, 1024], P('rep', 'fsdp'), as said below
- key_value_ckpt: float32 [2, 8192, 256], P('rep', 'fsdp'), as said below
- numerators: int32 [2], replicated, may hold values from 1 to 8
Outputs:
- context: bfloat16 [4096, 1024], P('fsdp')
Inputs may be any that keep to these rules, and one draw needn't show every extreme that they name: `tokens`: hidden states of mixed scales. `query_ckpt`: checkpoint weights. `key_value_ckpt`: checkpoint weights.
All inputs are finite; a program needn't handle non-finite values.
Results may differ from a plain program's by a relative error of at most 0.0081.
Values may be sent and summed in bfloat16 or wider, within the bound.
A program may use at most 128 MiB of HBM per device.

v0:
```python
import math

import jax
import jax.numpy as jnp
from jax import lax
from jax.sharding import PartitionSpec as P

theta_base = 500000.0
eps_norm = 1e-05
masked_score = -1e30


def rms_normed(hidden):
    wide_copy = hidden.astype(jnp.float32)
    return (
        wide_copy * lax.rsqrt(jnp.mean(wide_copy * wide_copy, axis=-1, keepdims=True) + eps_norm)
    ).astype(jnp.bfloat16)


def rotary(values, positions):
    half_size = values.shape[-1] // 2
    inverse_freq = jnp.exp(
        -(jnp.arange(half_size, dtype=jnp.float32) * (2.0 / values.shape[-1]))
        * math.log(theta_base)
    )
    angles = positions.astype(jnp.float32)[:, None] * inverse_freq[None, :]
    cosine_table = jnp.cos(angles)[:, None, :]
    sine_table = jnp.sin(angles)[:, None, :]
    first_half = values[..., :half_size]
    second_half = values[..., half_size:]
    return jnp.concatenate(
        [
            first_half * cosine_table - second_half * sine_table,
            second_half * cosine_table + first_half * sine_table,
        ],
        axis=-1,
    )


def attend_heads(queries, pair_rows, query_pos, key_pos):
    head_size = queries.shape[-1]
    key_rows = pair_rows[:, :head_size]
    value_rows = pair_rows[:, head_size:]
    score_scale = 1.0 / math.sqrt(head_size)
    allowed = key_pos[None, :] <= query_pos[:, None]

    def one_head(query_head):
        scores = jnp.dot(query_head, key_rows.T, preferred_element_type=jnp.float32) * score_scale
        scores = jnp.where(allowed, scores, masked_score)
        row_top = jnp.max(scores, axis=1, keepdims=True)
        weights_exp = jnp.exp(scores - row_top)
        norm_sum = jnp.sum(weights_exp, axis=1, keepdims=True)
        mixed_out = (
            jnp.dot(
                weights_exp.astype(jnp.bfloat16), value_rows, preferred_element_type=jnp.float32
            )
            / norm_sum
        )
        return mixed_out.astype(jnp.bfloat16)

    head_outs = lax.map(one_head, jnp.transpose(queries, (1, 0, 2)))
    return jnp.transpose(head_outs, (1, 0, 2)).reshape(queries.shape[0], -1)


def local(tokens, query_ckpt, key_value_ckpt, numerators):
    fsdp_count = lax.axis_size("fsdp")
    rep_idx = lax.axis_index("rep")
    fsdp_idx = lax.axis_index("fsdp")
    slot_ids = jnp.arange(numerators.shape[0], dtype=jnp.int32)
    weight_sum = jnp.sum(numerators).astype(jnp.float32)
    my_share = (
        jnp.sum(jnp.where(slot_ids == rep_idx, numerators, 0)).astype(jnp.float32) / weight_sum
    )
    query_term = my_share * query_ckpt[0]
    pair_term = my_share * key_value_ckpt[0]
    tok_dev = tokens.shape[0]
    seq_length = tok_dev * fsdp_count
    offset = fsdp_idx * tok_dev
    normed = rms_normed(tokens)
    query_width = query_ckpt.shape[2]
    pair_width = key_value_ckpt.shape[2]
    query_sum, pair_sum = lax.psum((query_term, pair_term), "rep")
    query_rows = query_sum.astype(jnp.bfloat16)
    pair_rows = pair_sum.astype(jnp.bfloat16)
    queries = jnp.dot(
        normed,
        lax.all_gather(query_rows, "fsdp", axis=0, tiled=True),
        preferred_element_type=jnp.float32,
    )
    pair_proj = jnp.dot(
        normed,
        lax.all_gather(pair_rows, "fsdp", axis=0, tiled=True),
        preferred_element_type=jnp.float32,
    )
    positions = (offset + jnp.arange(tok_dev, dtype=jnp.int32)) % seq_length
    head_size = pair_width // 2
    query_rot = rotary(
        queries.reshape(tok_dev, query_width // head_size, head_size), positions
    ).astype(jnp.bfloat16)
    key_rot = rotary(pair_proj[:, None, :head_size], positions)[:, 0, :].astype(jnp.bfloat16)
    pair_local = jnp.concatenate([key_rot, pair_proj[:, head_size:].astype(jnp.bfloat16)], axis=1)
    pair_all = lax.all_gather(pair_local, "fsdp", axis=0, tiled=True)
    key_pos = jnp.arange(seq_length, dtype=jnp.int32)
    context = attend_heads(query_rot, pair_all, positions, key_pos)
    return context


def solution(mesh):
    in_specs = (P("fsdp", None), P("rep", "fsdp", None), P("rep", "fsdp", None), P())
    out_specs = P("fsdp", None)
    return jax.shard_map(local, mesh=mesh, in_specs=in_specs, out_specs=out_specs, check_vma=False)
```

profile of v0, /device:TPU:29, one launch (start us, length us, event | category | flops | bytes accessed | tf_op | source)
XLA Modules:
  0.0 399.5 jit_solution(1901481260918514823)
XLA Ops:
  6.5 1.4 fusion.43
  9.3 1.8 multiply_bitcast_fusion
  11.1 11.2 %all-reduce.2 = (bf16[512,1024]{1,0:T(8,128)(2,1)}, bf16[512,256]{1,0:T(8,128)(2,1)}) all-reduce(f32[512,1024]{1,0:T(8,128)S(1)} %multiply_bitcast_fusion, f32[512,256]{1,0:T(8,128)S(1)} %multiply_bitcast_fusion.1), channel_id=1, replica_groups=mesh['rep'=2,'fsdp'=16] {'rep'}, use_global_device_ids=true, to_apply=%region_3.4 | all-reduce | flops 655360 | bytes 3932160 | tf_op jit(solution)/shard_map/psum | solution.py:82
  22.4 3.1 fusion.23
  25.5 72.1 %all-gather.6.cloned.1.call-done = bf16[8192,256]{1,0:T(8,128)(2,1)} async-done(((bf16[512,256]{1,0:T(8,128)(2,1)}), bf16[8192,256]{1,0:T(8,128)(2,1)}) %all-gather.6.cloned.1.call-update) | async-done | bytes 4194320 | tf_op jit(solution)/shard_map/all_gather | solution.py:92
  97.6 5.4 %fusion.25 = f32[256,256]{0,1:T(8,128)S(1)} fusion(bf16[8192,256]{1,0:T(8,128)(2,1)} %all-gather.6.cloned.1.call-done, bf16[256,8192]{1,0:T(8,128)(2,1)} %param.6, f32[256]{0:T(256)S(1)} %add_rsqrt_fusion), kind=kOutput, calls=%fused_computation.21 | convolution fusion | flops 1080033280 | bytes 8651776 | tf_op jit(solution)/shard_map/dot_general | solution.py:90
  105.3 61.0 %all-gather.8.cloned.1.call-done = bf16[4096,256]{0,1:T(8,128)(2,1)} async-done(((bf16[256,256]{0,1:T(8,128)(2,1)}), bf16[4096,256]{0,1:T(8,128)(2,1)}) %all-gather.8.cloned.1.call-update) | async-done | bytes 2097168 | tf_op jit(solution)/shard_map/all_gather | solution.py:102
  166.4 1.7 fusion.45
  169.4 191.0 %all-gather.4.cloned.1.call-done = bf16[8192,1024]{1,0:T(8,128)(2,1)} async-done(((bf16[512,1024]{1,0:T(8,128)(2,1)}), bf16[8192,1024]{1,0:T(8,128)(2,1)}) %all-gather.4.cloned.1.call-update) | async-done | bytes 16777232 | tf_op jit(solution)/shard_map/all_gather | solution.py:87
  360.4 9.5 %fusion.29 = f32[32,8,8,128]{3,1,2,0:T(8,128)S(1)} fusion(bf16[8192,1024]{1,0:T(8,128)(2,1)} %all-gather.4.cloned.1.call-done, bf16[256,8192]{1,0:T(8,128)(2,1)} %param.6, f32[256]{0:T(256)S(1)} %add_rsqrt_fusion), kind=kOutput, calls=%fused_computation.23 | convolution fusion | flops 4301258752 | bytes 22021120 | tf_op jit(solution)/shard_map/dot_general | solution.py:85
  371.2 20.8 %while.11 = (s32[]{:T(128)}, bf16[8,256,128]{2,1,0:T(8,128)(2,1)S(1)}, bf16[8,256,128]{2,1,0:T(8,128)(2,1)S(1)}, bf16[4096,128]{1,0:T(8,128)(2,1)S(1)}, bf16[409...) while((s32[]{:T(128)}, bf16[8,256,128]{2,1,0:T(8,128)(2,1)S(1)}, ...), condition=%wide.region_8.9_spmd.clone, body=%wide.region_5.8_spmd.clone.sunk | while | flops 545324544 | bytes 14817365 | solution.py:61
  371.3 1.0 fusion.61
  372.2 0.7 fusion.62
  372.9 0.9 fusion.63
  373.9 1.0 fusion.61
  374.8 0.7 fusion.62
  375.5 0.9 fusion.63
  376.5 1.0 fusion.61
  377.4 0.7 fusion.62
  378.1 0.9 fusion.63
  379.1 1.0 fusion.61
  380.0 0.7 fusion.62
  380.7 0.9 fusion.63
  381.7 1.0 fusion.61
  383.3 0.9 fusion.63
  384.3 1.0 fusion.61
  385.9 0.9 fusion.63
  386.9 1.0 fusion.61
  388.5 0.9 fusion.63
  389.5 1.0 fusion.61
  391.1 0.9 fusion.63
  392.1 0.9 copy_bitcast_fusion
  (32 shorter events, 7.9 us)
Async XLA Ops:
  6.5 4.5 %copy-start.1 = (f32[1,512,256]{2,1,0:T(8,128)S(1)}, f32[1,512,256]{2,1,0:T(8,128)}, u32[]{:S(2)}) copy-start(f32[1,512,256]{2,1,0:T(8,128)} %param.8) | copy-start | bytes 1572868
  6.5 91.0 %all-gather.6.cloned.1.call-start = ((), (), s32[]{:S(2)}) async-start(), calls=%async_computation.1 | async-start | bytes 4456448 | tf_op jit(solution)/shard_map/all_gather | solution.py:92
  22.3 144.1 %all-gather.8.cloned.1.call-start = ((), (), s32[]{:S(2)}) async-start(), calls=%async_computation.2 | async-start | bytes 2228224 | tf_op jit(solution)/shard_map/all_gather | solution.py:102
  104.0 256.4 %all-gather.4.cloned.1.call-start = ((), (), s32[]{:S(2)}) async-start(), calls=%async_computation | async-start | bytes 17825792 | tf_op jit(solution)/shard_map/all_gather | solution.py:87
  370.2 1.1 copy-start
Sparse Core Ops, SparseCore 0:
  22.4 75.1 all-gather.5
  104.1 62.1 all-gather.7
  169.1 191.2 all-gather.3
where the time goes:
time: 403 us; the launch traced here: 399 us
  waiting for transfers between devices  325 us (81%)
  matrix products  29.9 us (7%)
  between operations  14.6 us (4%)
  other arithmetic  14.3 us (4%)
  blocking collectives  11.2 us (3%)
  local copies, waits for them, and re-layouts  4.44 us (1%)
    all_gather x1, waiting for transfers between devices, local(): lax.all_gather(query_rows, 'fsdp', axis=0, tiled=True)  191 us
    all_gather x1, waiting for transfers between devices, local(): lax.all_gather(pair_rows, 'fsdp', axis=0, tiled=True)  72.1 us
    all_gather x1, waiting for transfers between devices, local(): pair_all = lax.all_gather(pair_local, 'fsdp', axis=0, tiled=True)  61 us
    psum x1, blocking collectives, local(): query_sum, pair_sum = lax.psum((query_term, pair_term), 'rep')  11.2 us
    dot_general x1, matrix products, local(): jnp.dot(normed, lax.all_gather(query_rows, 'fsdp', axis=0, tiled=True), p...  9.53 us
  transfers between devices with their start and end apart: 3, of which 3 were waited for; matrix products, arithmetic and copies ran while one was open for 2% of the time, Pallas kernels for 0%

commit v1 on v0

--- a/solution.py
+++ b/solution.py
@@ -1,8 +1,12 @@
 import math
+
+import functools
 
 import jax
 import jax.numpy as jnp
 from jax import lax
+from jax.experimental import pallas as pl
+from jax.experimental.pallas import tpu as pltpu
 from jax.sharding import PartitionSpec as P
 
 theta_base = 500000.0
@@ -105,7 +109,445 @@
     return context
 
 
+MESH = pl.DeviceIdType.MESH
+plane = 4
+
+
+def fused_kernel(
+    n_line, share_ref, cos_ref, sin_ref, tok_hbm, query_hbm, pair_hbm, out_ref,
+    raw, nrm, mine, theirs, wbuf, tok, acc, rsend, rrecv, qrot, kvb,
+    raw_sem, mine_sem, ck_s, ck_r, w_s, w_r, tl_sem, tp_s, tp_r, ts_s, ts_r,
+    rs_s, rs_r, kz_s, kp_s, kb_s, kz_r, ks_r, o_s, o_r,
+):
+    n_fsdp = n_line * plane
+    r = lax.axis_index("rep")
+    f = lax.axis_index("fsdp")
+    z, p = f // plane, lax.rem(f, plane)
+    sib = 1 - r
+    n_heads = qrot.shape[0]
+    pieces = n_heads + 1
+    n_tok = acc.shape[1]
+    half = n_tok // 2
+    head = acc.shape[2]
+    depth = wbuf.shape[2]
+    can_up, can_down = z < n_line - 1, z > 0
+    to_sib = {"rep": sib}
+
+    def peer(j):
+        return lax.rem(p + j, plane)
+
+    def remote(src, dst, send, recv, where):
+        return pltpu.make_async_remote_copy(
+            src_ref=src, dst_ref=dst, send_sem=send, recv_sem=recv,
+            device_id=where, device_id_type=MESH,
+        )
+
+    def others(fn):
+        for d in range(1, n_line):
+            pl.when(z >= d)(functools.partial(fn, z - d, True))
+            pl.when(z + d < n_line)(functools.partial(fn, z + d, False))
+
+    raw_copy = pltpu.make_async_copy(
+        tok_hbm.at[pl.ds(pl.multiple_of(r * half, half), half), :], raw, raw_sem
+    )
+
+    def columns(k, side):
+        if k == 0:
+            return pair_hbm.at[0, :, pl.ds(pl.multiple_of(side * head, head), head)]
+        first = pl.multiple_of((side * n_heads + (k - 1)) * head, head)
+        return query_hbm.at[0, :, pl.ds(first, head)]
+
+    def own_ckpt(k):
+        return pltpu.make_async_copy(columns(k, r), mine.at[k], mine_sem.at[k])
+
+    def sib_ckpt(k):
+        return remote(columns(k, sib), theirs.at[k], ck_s.at[k], ck_r.at[k], to_sib)
+
+    own_ckpt(0).start()
+    raw_copy.start()
+    for k in range(1, pieces):
+        own_ckpt(k).start()
+
+    barrier = pltpu.get_barrier_semaphore()
+    pl.semaphore_signal(barrier, inc=1, device_id=to_sib, device_id_type=MESH)
+    for j in range(1, plane):
+        pl.semaphore_signal(
+            barrier, inc=1, device_id={"fsdp": z * plane + peer(j)}, device_id_type=MESH
+        )
+
+    @pl.when(can_up)
+    def _():
+        pl.semaphore_signal(barrier, inc=1, device_id={"fsdp": f + plane}, device_id_type=MESH)
+
+    @pl.when(can_down)
+    def _():
+        pl.semaphore_signal(barrier, inc=1, device_id={"fsdp": f - plane}, device_id_type=MESH)
+
+    pl.semaphore_wait(barrier, plane + can_up.astype(jnp.int32) + can_down.astype(jnp.int32))
+
+    for k in range(pieces):
+        sib_ckpt(k).start()
+
+    def w_copy(k, c, up):
+        return remote(
+            wbuf.at[k, c], wbuf.at[k, c], w_s.at[k, c, 0 if up else 1], w_r.at[k, c],
+            {"fsdp": f + plane if up else f - plane},
+        )
+
+    def average(k):
+        own_ckpt(k).wait()
+        sib_ckpt(k).wait_recv()
+        wbuf[k, z] = (share_ref[r] * mine[k] + share_ref[sib] * theirs[k]).astype(jnp.bfloat16)
+
+    def send_own(k):
+        pl.when(can_up)(lambda: w_copy(k, z, True).start())
+        pl.when(can_down)(lambda: w_copy(k, z, False).start())
+
+    def forward(k):
+        def one(c, from_below):
+            w_copy(k, c, from_below).wait_recv()
+            pl.when(can_up if from_below else can_down)(lambda: w_copy(k, c, from_below).start())
+
+        others(one)
+
+    average(0)
+    send_own(0)
+
+    raw_copy.wait()
+
+    def norm_rows(i, carry):
+        rows = pl.ds(pl.multiple_of(i * 16, 16), 16)
+        wide = raw[rows, :].astype(jnp.float32)
+        inv = lax.rsqrt(jnp.mean(wide * wide, axis=-1, keepdims=True) + eps_norm)
+        for b in range(n_fsdp):
+            part = raw[rows, b * depth : (b + 1) * depth].astype(jnp.float32)
+            nrm[b, rows, :] = (part * inv).astype(jnp.bfloat16)
+        return carry
+
+    lax.fori_loop(0, half // 16, norm_rows, 0)
+
+    def tok_rows(c, chip, side):
+        first = pl.multiple_of(chip * n_tok + side * half, half)
+        return tok.at[c, pl.ds(first, half), :]
+
+    def tok_own(c):
+        return pltpu.make_async_copy(nrm.at[c * plane + p], tok_rows(c, p, r), tl_sem.at[c])
+
+    def tok_own_sib(c):
+        return remote(
+            nrm.at[c * plane + p], tok_rows(c, p, r), ts_s.at[c, p], ts_r.at[c, p], to_sib
+        )
+
+    def tok_peer(c, j):
+        q = peer(j)
+        return remote(
+            nrm.at[c * plane + q], tok_rows(c, p, r), tp_s.at[c, q], tp_r.at[c, p],
+            {"fsdp": z * plane + q},
+        )
+
+    def tok_arrival(c, j):
+        q = peer(j)
+        return remote(tok_rows(c, q, r), tok_rows(c, q, r), tp_s.at[c, q], tp_r.at[c, q], to_sib)
+
+    def tok_pass(c, j):
+        q = peer(j)
+        return remote(tok_rows(c, q, r), tok_rows(c, q, r), ts_s.at[c, q], ts_r.at[c, q], to_sib)
+
+    def tok_from_sib(c, q):
+        return remote(
+            tok_rows(c, q, sib), tok_rows(c, q, sib), ts_s.at[c, q], ts_r.at[c, q], to_sib
+        )
+
+    for c in range(n_line):
+        for j in range(1, plane):
+            tok_peer(c, j).start()
+        tok_own(c).start()
+        tok_own_sib(c).start()
+
+    for k in range(1, pieces):
+        average(k)
+        if k <= 2:
+            send_own(k)
+
+    forward(0)
+    send_own(3)
+    forward(1)
+    send_own(4)
+
+    for c in range(n_line):
+        for j in range(1, plane):
+            tok_arrival(c, j).wait_recv()
+            tok_pass(c, j).start()
+    for c in range(n_line):
+        tok_own(c).wait()
+        for q in range(plane):
+            tok_from_sib(c, q).wait_recv()
+
+    def rs_copy(k, j):
+        q = peer(j)
+        return remote(
+            rsend.at[k, q], rrecv.at[k, p], rs_s.at[k, q], rs_r.at[k, p],
+            {"fsdp": z * plane + q},
+        )
+
+    def rs_arrival(k, j):
+        q = peer(j)
+        return remote(rrecv.at[k, q], rrecv.at[k, q], rs_s.at[k, q], rs_r.at[k, q], to_sib)
+
+    def multiply(k):
+        for j in (2, 1, 3, 0):
+            q = peer(j)
+            rows = pl.ds(pl.multiple_of(q * n_tok, n_tok), n_tok)
+            part = jnp.dot(tok[0, rows, :], wbuf[k, 0], preferred_element_type=jnp.float32)
+            for c in range(1, n_line):
+                part += jnp.dot(tok[c, rows, :], wbuf[k, c], preferred_element_type=jnp.float32)
+            if j:
+                rsend[k, q] = part.astype(jnp.bfloat16)
+                rs_copy(k, j).start()
+            else:
+                acc[k] = part
+
+    def total(k):
+        value = acc[k]
+        for j in range(1, plane):
+            rs_arrival(k, j).wait_recv()
+            value += rrecv[k, peer(j)].astype(jnp.float32)
+        return value
+
+    def rotate(value):
+        return value * cos_ref[...] + pltpu.roll(value, head // 2, 1) * sin_ref[...]
+
+    def kv_rows(b, side):
+        return kvb.at[side, pl.ds(pl.multiple_of(b * n_tok, n_tok), n_tok), :]
+
+    def kv_line(c, up):
+        b = c * plane + p
+        return remote(
+            kv_rows(b, r), kv_rows(b, r), kz_s.at[c, 0 if up else 1], kz_r.at[b],
+            {"fsdp": f + plane if up else f - plane},
+        )
+
+    def kv_plane(c, j):
+        b = c * plane + p
+        return remote(
+            kv_rows(b, r), kv_rows(b, r), kp_s.at[c, peer(j)], kz_r.at[b],
+            {"fsdp": z * plane + peer(j)},
+        )
+
+    def kv_sib(b):
+        return remote(kv_rows(b, r), kv_rows(b, r), kb_s.at[b], ks_r.at[b], to_sib)
+
+    def kv_from_sib(b):
+        return remote(kv_rows(b, sib), kv_rows(b, sib), kb_s.at[b], ks_r.at[b], to_sib)
+
+    def kv_arrival(b):
+        return remote(kv_rows(b, r), kv_rows(b, r), kb_s.at[b], kz_r.at[b], to_sib)
+
+    def kv_spread(c):
+        for j in range(1, plane):
+            kv_plane(c, j).start()
+        kv_sib(c * plane + p).start()
+
+    def kv_begin():
+        value = total(0)
+        value = jnp.where(r == 0, rotate(value), value)
+        kvb[r, pl.ds(pl.multiple_of(f * n_tok, n_tok), n_tok), :] = value.astype(jnp.bfloat16)
+        pl.when(can_up)(lambda: kv_line(z, True).start())
+        pl.when(can_down)(lambda: kv_line(z, False).start())
+        kv_spread(z)
+
+    def kv_middle():
+        def one(c, from_below):
+            kv_arrival(c * plane + p).wait_recv()
+            pl.when(can_up if from_below else can_down)(lambda: kv_line(c, from_below).start())
+            kv_spread(c)
+
+        others(one)
+
+    def kv_end():
+        for c in range(n_line):
+            for j in range(1, plane):
+                b = c * plane + peer(j)
+                kv_arrival(b).wait_recv()
+                kv_sib(b).start()
+        for b in range(n_fsdp):
+            kv_from_sib(b).wait_recv()
+
+    block = 2 * n_tok
+    scale = math.log2(math.e) / math.sqrt(head)
+
+    def out_copy(h, side):
+        col = pl.ds(pl.multiple_of((side * n_heads + h) * head, head), head)
+        return remote(out_ref.at[:, col], out_ref.at[:, col], o_s.at[h], o_r.at[h], to_sib)
+
+    def query(h):
+        qrot[h] = rotate(total(h + 1)).astype(jnp.bfloat16)
+
+    def attend(h):
+        q = qrot[h]
+
+        def step(i, carry, masked):
+            top, norm, mixed = carry
+            rows = pl.ds(pl.multiple_of(i * block, block), block)
+            scores = lax.dot_general(
+                q, kvb[0, rows, :], (((1,), (1,)), ((), ())), preferred_element_type=jnp.float32
+            )
+            if masked:
+                row = lax.broadcasted_iota(jnp.int32, scores.shape, 0) + f * n_tok
+                col = lax.broadcasted_iota(jnp.int32, scores.shape, 1) + i * block
+                scores = jnp.where(col <= row, scores, masked_score)
+            new_top = jnp.maximum(top, jnp.max(scores, axis=1, keepdims=True))
+            weights = jnp.exp2((scores - new_top) * scale)
+            fade = jnp.exp2((top - new_top) * scale)
+            norm = norm * fade + jnp.sum(weights, axis=1, keepdims=True)
+            mixed = mixed * fade + jnp.dot(
+                weights.astype(jnp.bfloat16), kvb[1, rows, :], preferred_element_type=jnp.float32
+            )
+            return new_top, norm, mixed
+
+        last = (f * n_tok) // block
+        carry = (
+            jnp.full((n_tok, 1), masked_score, jnp.float32),
+            jnp.zeros((n_tok, 1), jnp.float32),
+            jnp.zeros((n_tok, head), jnp.float32),
+        )
+        carry = step(last, carry, True)
+        _, norm, mixed = lax.fori_loop(0, last, functools.partial(step, masked=False), carry)
+        col = pl.ds(pl.multiple_of((r * n_heads + h) * head, head), head)
+        out_ref[:, col] = (mixed / norm).astype(jnp.bfloat16)
+        out_copy(h, r).start()
+
+    multiply(0)
+    multiply(1)
+    kv_begin()
+    forward(2)
+    multiply(2)
+    kv_middle()
+    forward(3)
+    multiply(3)
+    query(0)
+    query(1)
+    kv_end()
+    attend(0)
+    forward(4)
+    multiply(4)
+    attend(1)
+    query(2)
+    attend(2)
+    query(3)
+    attend(3)
+
+    for k in range(pieces):
+        sib_ckpt(k).wait_send()
+        pl.when(can_up)(lambda k=k: w_copy(k, z, True).wait_send())
+        pl.when(can_down)(lambda k=k: w_copy(k, z, False).wait_send())
+
+        def sent(c, from_below, k=k):
+            ok = can_up if from_below else can_down
+            pl.when(ok)(lambda: w_copy(k, c, from_below).wait_send())
+
+        others(sent)
+        for j in range(1, plane):
+            rs_copy(k, j).wait_send()
+    for c in range(n_line):
+        tok_own_sib(c).wait_send()
+        for j in range(1, plane):
+            tok_peer(c, j).wait_send()
+            tok_pass(c, j).wait_send()
+            kv_plane(c, j).wait_send()
+    pl.when(can_up)(lambda: kv_line(z, True).wait_send())
+    pl.when(can_down)(lambda: kv_line(z, False).wait_send())
+
+    def kv_sent(c, from_below):
+        ok = can_up if from_below else can_down
+        pl.when(ok)(lambda: kv_line(c, from_below).wait_send())
+
+    others(kv_sent)
+    for b in range(n_fsdp):
+        kv_sib(b).wait_send()
+    for h in range(n_heads):
+        out_copy(h, r).wait_send()
+        out_copy(h, sib).wait_recv()
+
+
+def fused_local(tokens, query_ckpt, key_value_ckpt, numerators):
+    n_fsdp = lax.axis_size("fsdp")
+    n_line = n_fsdp // plane
+    n_tok, width = tokens.shape
+    depth, query_width = query_ckpt.shape[1:]
+    head = key_value_ckpt.shape[2] // 2
+    n_heads = query_width // head // 2
+    pieces = n_heads + 1
+    half = n_tok // 2
+    shares = numerators.astype(jnp.float32) / jnp.sum(numerators).astype(jnp.float32)
+    positions = lax.axis_index("fsdp") * n_tok + jnp.arange(n_tok, dtype=jnp.int32)
+    inverse_freq = jnp.exp(
+        -(jnp.arange(head // 2, dtype=jnp.float32) * (2.0 / head)) * math.log(theta_base)
+    )
+    angles = positions.astype(jnp.float32)[:, None] * inverse_freq[None, :]
+    cosine, sine = jnp.cos(angles), jnp.sin(angles)
+    cos_table = jnp.concatenate([cosine, cosine], axis=1)
+    sin_table = jnp.concatenate([-sine, sine], axis=1)
+    vmem, bf16, f32 = pltpu.VMEM, jnp.bfloat16, jnp.float32
+    dma = pltpu.SemaphoreType.DMA
+    return pl.pallas_call(
+        functools.partial(fused_kernel, n_line),
+        out_shape=jax.ShapeDtypeStruct((n_tok, query_width), bf16),
+        in_specs=[
+            pl.BlockSpec(memory_space=pltpu.SMEM),
+            pl.BlockSpec(memory_space=pltpu.VMEM),
+            pl.BlockSpec(memory_space=pltpu.VMEM),
+            pl.BlockSpec(memory_space=pl.ANY),
+            pl.BlockSpec(memory_space=pl.ANY),
+            pl.BlockSpec(memory_space=pl.ANY),
+        ],
+        out_specs=pl.BlockSpec(memory_space=pltpu.VMEM),
+        scratch_shapes=[
+            vmem((half, width), bf16),
+            vmem((n_fsdp, half, depth), bf16),
+            vmem((pieces, depth, head), f32),
+            vmem((pieces, depth, head), f32),
+            vmem((pieces, n_line, depth, head), bf16),
+            vmem((n_line, plane * n_tok, depth), bf16),
+            vmem((pieces, n_tok, head), f32),
+            vmem((pieces, plane, n_tok, head), bf16),
+            vmem((pieces, plane, n_tok, head), bf16),
+            vmem((n_heads, n_tok, head), bf16),
+            vmem((2, n_fsdp * n_tok, head), bf16),
+            dma,
+            dma((pieces,)),
+            dma((pieces,)),
+            dma((pieces,)),
+            dma((pieces, n_line, 2)),
+            dma((pieces, n_line)),
+            dma((n_line,)),
+            dma((n_line, plane)),
+            dma((n_line, plane)),
+            dma((n_line, plane)),
+            dma((n_line, plane)),
+            dma((pieces, plane)),
+            dma((pieces, plane)),
+            dma((n_line, 2)),
+            dma((n_line, plane)),
+            dma((n_fsdp,)),
+            dma((n_fsdp,)),
+            dma((n_fsdp,)),
+            dma((n_heads,)),
+            dma((n_heads,)),
+        ],
+        compiler_params=pltpu.CompilerParams(
+            collective_id=0, has_side_effects=True, vmem_limit_bytes=48 * 1024 * 1024
+        ),
+        cost_estimate=pl.CostEstimate(
+            flops=2 * n_tok * width * query_width, bytes_accessed=8 * depth * query_width,
+            transcendentals=n_heads * n_tok * n_tok * n_fsdp,
+        ),
+    )(shares, cos_table, sin_table, tokens, query_ckpt, key_value_ckpt)
+
+
 def solution(mesh):
     in_specs = (P("fsdp", None), P("rep", "fsdp", None), P("rep", "fsdp", None), P())
     out_specs = P("fsdp", None)
-    return jax.shard_map(local, mesh=mesh, in_specs=in_specs, out_specs=out_specs, check_vma=False)
+    paired = mesh.shape["rep"] == 2 and mesh.shape["fsdp"] % plane == 0
+    body = fused_local if paired else local
+    return jax.shard_map(body, mesh=mesh, in_specs=in_specs, out_specs=out_specs, check_vma=False)

time: 403 us -> 93.1 us (0.23)
  waiting for transfers between devices: 325 us -> 0 us
  Pallas kernels: 0 us -> 86.1 us
  matrix products: 29.9 us -> 0 us
  between operations: 14.6 us -> 0.69 us
  other arithmetic: 14.3 us -> 2.65 us
  blocking collectives: 11.2 us -> 0 us
    all_gather x3 -> x0, waiting for transfers between devices: 324 us -> none  [the longest x1 191 us: local(): lax.all_gather(query_rows, 'fsdp', axis=0, tiled=True)]
    pallas_call x0 -> x1, Pallas kernels: none -> 86.1 us  [fused_local(): pl.pallas_call(functools.partial(fused_kernel, n_line), out_shape=jax.Sha...]
    dot_general x18 -> x0, matrix products: 29.9 us -> none  [the longest x1 9.53 us: local(): jnp.dot(normed, lax.all_gather(query_rows, 'fsdp', axis=0, tiled=True), p...]
    psum x1 -> x0, blocking collectives: 11.2 us -> none  [local(): query_sum, pair_sum = lax.psum((query_term, pair_term), 'rep')]
    reduce_sum x10 -> x1, other arithmetic: 10.3 us -> 1.29 us  [fused_local(): jnp.sum(numerators).astype(jnp.float32)]
  transfers between devices with their start and end apart: 3 -> 0, of which waited for: 3 -> 0; matrix products, arithmetic and copies ran while one was open for 2% -> 0% of each run, Pallas kernels for 0% -> 0%
where the time goes in v1:
time: 93.1 us; the launch traced here: 92.8 us
  Pallas kernels  86.1 us (92%)
  local copies, waits for them, and re-layouts  3.42 us (4%)
  other arithmetic  2.65 us (3%)
    pallas_call x1, Pallas kernels, fused_local(): pl.pallas_call(functools.partial(fused_kernel, n_line), out_shape=jax.Sha...  86.1 us
    unnamed x5, local copies, waits for them, and re-layouts  3.42 us

profile of v1, /device:TPU:29, one launch (start us, length us, event | category | flops | bytes accessed | tf_op | source)
XLA Modules:
  0.0 92.8 jit_solution(13884744966051860728)
XLA Ops:
  0.0 1.3 %reduce_sum.9 = s32[]{:T(128)} reduce(s32[2]{0:T(128)} %param.7, s32[]{:T(128)} %constant.5.clone.1), dimensions={0}, to_apply=%region_0.0 | reduce | flops 1 | bytes 16 | tf_op jit(solution)/shard_map/reduce_sum | solution.py:482
  1.9 0.7 convert_divide_fusion.share_ref
  2.6 0.5 fusion
  3.2 0.1 pad_maximum_fusion
  3.3 0.0 copy-start
  3.3 1.6 %copy-done = f32[1,512,1024]{2,1,0:T(8,128)S(1)} copy-done((f32[1,512,1024]{2,1,0:T(8,128)S(1)}, f32[1,512,1024]{2,1,0:T(8,128)}, u32[]{:S(2)}) %copy-start) | copy-done | bytes 2097176
  4.9 0.0 copy-start.1
  4.9 1.0 %copy-done.1 = f32[1,512,256]{2,1,0:T(8,128)S(1)} copy-done((f32[1,512,256]{2,1,0:T(8,128)S(1)}, f32[1,512,256]{2,1,0:T(8,128)}, u32[]{:S(2)}) %copy-start.1) | copy-done | bytes 524312
  6.0 86.1 %shard_map.46 = bf16[256,1024]{1,0:T(8,128)(2,1)S(1)} custom-call(f32[2]{0:T(128)S(1)} %convert_divide_fusion.share_ref, f32[256,128]{1,0:T(8,128)S(1)} %get-tuple-element.8.cos_ref, f32[256,128]{1,0:T(8,128)S(1)} %get-tuple-element.9.sin_ref, bf16[256,8192]{1,0:T(8,128)(2,1)} %tok_hbm.1, f32[1,512,1024]{2,1,0:T(8,128)S(1)} %copy-done, ...), custom_call_target="tpu_custom_call" | custom-call | flops 4294967296 | bytes 4194304 | tf_op jit(solution)/shard_map/pallas_call | solution.py:493
  92.0 0.8 copy.6
  (2 shorter events, 0.0 us)
Async XLA Ops:
  3.3 1.6 %copy-start = (f32[1,512,1024]{2,1,0:T(8,128)S(1)}, f32[1,512,1024]{2,1,0:T(8,128)}, u32[]{:S(2)}) copy-start(f32[1,512,1024]{2,1,0:T(8,128)} %query_hbm.1) | copy-start | bytes 6291460
  4.9 1.0 %copy-start.1 = (f32[1,512,256]{2,1,0:T(8,128)S(1)}, f32[1,512,256]{2,1,0:T(8,128)}, u32[]{:S(2)}) copy-start(f32[1,512,256]{2,1,0:T(8,128)} %pair_hbm.1) | copy-start | bytes 1572868

commit v2 on v1

--- a/solution.py
+++ b/solution.py
@@ -114,8 +114,8 @@
 
 
 def fused_kernel(
-    n_line, share_ref, cos_ref, sin_ref, tok_hbm, query_hbm, pair_hbm, out_ref,
-    raw, nrm, mine, theirs, wbuf, tok, acc, rsend, rrecv, qrot, kvb,
+    n_line, num_ref, cos_ref, sin_ref, tok_hbm, query_hbm, pair_hbm, out_ref,
+    raw, inv_rms, nrm, mine, theirs, wbuf, tok, acc, rsend, rrecv, qrot, kvb,
     raw_sem, mine_sem, ck_s, ck_r, w_s, w_r, tl_sem, tp_s, tp_r, ts_s, ts_r,
     rs_s, rs_r, kz_s, kp_s, kb_s, kz_r, ks_r, o_s, o_r,
 ):
@@ -142,8 +142,8 @@
             device_id=where, device_id_type=MESH,
         )
 
-    def others(fn):
-        for d in range(1, n_line):
+    def others(fn, lo=1, hi=n_line):
+        for d in range(lo, hi):
             pl.when(z >= d)(functools.partial(fn, z - d, True))
             pl.when(z + d < n_line)(functools.partial(fn, z + d, False))
 
@@ -194,90 +194,118 @@
             {"fsdp": f + plane if up else f - plane},
         )
 
+    def share(side):
+        whole = (num_ref[0] + num_ref[1]).astype(jnp.float32)
+        return jnp.full((1, head), num_ref[side].astype(jnp.float32)) / jnp.full((1, head), whole)
+
     def average(k):
         own_ckpt(k).wait()
         sib_ckpt(k).wait_recv()
-        wbuf[k, z] = (share_ref[r] * mine[k] + share_ref[sib] * theirs[k]).astype(jnp.bfloat16)
+        wbuf[k, z] = (share(r) * mine[k] + share(sib) * theirs[k]).astype(jnp.bfloat16)
 
     def send_own(k):
         pl.when(can_up)(lambda: w_copy(k, z, True).start())
         pl.when(can_down)(lambda: w_copy(k, z, False).start())
 
-    def forward(k):
+    def forward(k, lo=1, hi=n_line):
         def one(c, from_below):
             w_copy(k, c, from_below).wait_recv()
             pl.when(can_up if from_below else can_down)(lambda: w_copy(k, c, from_below).start())
 
-        others(one)
-
-    average(0)
-    send_own(0)
-
-    raw_copy.wait()
-
-    def norm_rows(i, carry):
+        others(one, lo, hi)
+
+    def near(k):
+        forward(k, 1, min(2, n_line))
+
+    def middle(k):
+        forward(k, 2, n_line - 1)
+
+    def far(k):
+        forward(k, max(2, n_line - 1), n_line)
+
+    def tok_rows(c, chip, side):
+        first = pl.multiple_of(chip * n_tok + side * half, half)
+        return tok.at[c, pl.ds(first, half), :]
+
+    def tok_own(c):
+        return pltpu.make_async_copy(nrm.at[c * plane + p], tok_rows(c, p, r), tl_sem.at[c])
+
+    def tok_own_sib(c):
+        return remote(
+            nrm.at[c * plane + p], tok_rows(c, p, r), ts_s.at[c, p], ts_r.at[c, p], to_sib
+        )
+
+    def tok_peer(c, j):
+        q = peer(j)
+        return remote(
+            nrm.at[c * plane + q], tok_rows(c, p, r), tp_s.at[c, q], tp_r.at[c, p],
+            {"fsdp": z * plane + q},
+        )
+
+    def tok_arrival(c, j):
+        q = peer(j)
+        return remote(tok_rows(c, q, r), tok_rows(c, q, r), tp_s.at[c, q], tp_r.at[c, q], to_sib)
+
+    def tok_pass(c, j):
+        q = peer(j)
+        return remote(tok_rows(c, q, r), tok_rows(c, q, r), ts_s.at[c, q], ts_r.at[c, q], to_sib)
+
+    def tok_from_sib(c, q):
+        return remote(
+            tok_rows(c, q, sib), tok_rows(c, q, sib), ts_s.at[c, q], ts_r.at[c, q], to_sib
+        )
+
+    def inverse_rms(i, carry):
         rows = pl.ds(pl.multiple_of(i * 16, 16), 16)
         wide = raw[rows, :].astype(jnp.float32)
         inv = lax.rsqrt(jnp.mean(wide * wide, axis=-1, keepdims=True) + eps_norm)
-        for b in range(n_fsdp):
-            part = raw[rows, b * depth : (b + 1) * depth].astype(jnp.float32)
-            nrm[b, rows, :] = (part * inv).astype(jnp.bfloat16)
+        inv_rms[rows, :] = jnp.broadcast_to(inv, (16, inv_rms.shape[1]))
         return carry
 
-    lax.fori_loop(0, half // 16, norm_rows, 0)
-
-    def tok_rows(c, chip, side):
-        first = pl.multiple_of(chip * n_tok + side * half, half)
-        return tok.at[c, pl.ds(first, half), :]
-
-    def tok_own(c):
-        return pltpu.make_async_copy(nrm.at[c * plane + p], tok_rows(c, p, r), tl_sem.at[c])
-
-    def tok_own_sib(c):
-        return remote(
-            nrm.at[c * plane + p], tok_rows(c, p, r), ts_s.at[c, p], ts_r.at[c, p], to_sib
-        )
-
-    def tok_peer(c, j):
-        q = peer(j)
-        return remote(
-            nrm.at[c * plane + q], tok_rows(c, p, r), tp_s.at[c, q], tp_r.at[c, p],
-            {"fsdp": z * plane + q},
-        )
-
-    def tok_arrival(c, j):
-        q = peer(j)
-        return remote(tok_rows(c, q, r), tok_rows(c, q, r), tp_s.at[c, q], tp_r.at[c, q], to_sib)
-
-    def tok_pass(c, j):
-        q = peer(j)
-        return remote(tok_rows(c, q, r), tok_rows(c, q, r), ts_s.at[c, q], ts_r.at[c, q], to_sib)
-
-    def tok_from_sib(c, q):
-        return remote(
-            tok_rows(c, q, sib), tok_rows(c, q, sib), ts_s.at[c, q], ts_r.at[c, q], to_sib
-        )
-
-    for c in range(n_line):
-        for j in range(1, plane):
+    def norm_send(c):
+        def norm_rows(i, carry):
+            rows = pl.ds(pl.multiple_of(i * 16, 16), 16)
+            inv = inv_rms[rows, :1]
+            for b in range(c * plane, (c + 1) * plane):
+                part = raw[rows, b * depth : (b + 1) * depth].astype(jnp.float32)
+                nrm[b, rows, :] = (part * inv).astype(jnp.bfloat16)
+            return carry
+
+        lax.fori_loop(0, half // 16, norm_rows, 0)
+        for j in (2, 1, 3):
             tok_peer(c, j).start()
         tok_own(c).start()
         tok_own_sib(c).start()
 
-    for k in range(1, pieces):
-        average(k)
-        if k <= 2:
-            send_own(k)
-
-    forward(0)
-    send_own(3)
-    forward(1)
-    send_own(4)
-
-    for c in range(n_line):
+    def tok_collect(c):
         for j in range(1, plane):
             tok_arrival(c, j).wait_recv()
             tok_pass(c, j).start()
+
+    average(0)
+    send_own(0)
+    raw_copy.wait()
+    lax.fori_loop(0, half // 16, inverse_rms, 0)
+    average(1)
+    send_own(1)
+    norm_send(0)
+    near(0)
+    for k in range(2, pieces):
+        average(k)
+        send_own(k)
+        if k - 1 < n_line:
+            norm_send(k - 1)
+    for c in range(pieces - 1, n_line):
+        norm_send(c)
+    middle(0)
+    for k in range(1, pieces):
+        near(k)
+    for c in range(n_line):
+        tok_collect(c)
+        if c + 1 < pieces:
+            middle(c + 1)
+    for k in range(n_line + 1, pieces):
+        middle(k)
     for c in range(n_line):
         tok_own(c).wait()
         for q in range(plane):
@@ -356,13 +384,13 @@
         pl.when(can_down)(lambda: kv_line(z, False).start())
         kv_spread(z)
 
-    def kv_middle():
+    def kv_step(lo, hi):
         def one(c, from_below):
             kv_arrival(c * plane + p).wait_recv()
             pl.when(can_up if from_below else can_down)(lambda: kv_line(c, from_below).start())
             kv_spread(c)
 
-        others(one)
+        others(one, lo, hi)
 
     def kv_end():
         for c in range(n_line):
@@ -417,22 +445,25 @@
         out_ref[:, col] = (mixed / norm).astype(jnp.bfloat16)
         out_copy(h, r).start()
 
+    far(0)
     multiply(0)
+    far(1)
     multiply(1)
     kv_begin()
-    forward(2)
+    far(2)
     multiply(2)
-    kv_middle()
-    forward(3)
+    kv_step(1, min(2, n_line))
+    far(3)
     multiply(3)
+    kv_step(2, n_line)
+    far(4)
+    multiply(4)
     query(0)
     query(1)
+    query(2)
     kv_end()
     attend(0)
-    forward(4)
-    multiply(4)
     attend(1)
-    query(2)
     attend(2)
     query(3)
     attend(3)
@@ -479,7 +510,6 @@
     n_heads = query_width // head // 2
     pieces = n_heads + 1
     half = n_tok // 2
-    shares = numerators.astype(jnp.float32) / jnp.sum(numerators).astype(jnp.float32)
     positions = lax.axis_index("fsdp") * n_tok + jnp.arange(n_tok, dtype=jnp.int32)
     inverse_freq = jnp.exp(
         -(jnp.arange(head // 2, dtype=jnp.float32) * (2.0 / head)) * math.log(theta_base)
@@ -504,6 +534,7 @@
         out_specs=pl.BlockSpec(memory_space=pltpu.VMEM),
         scratch_shapes=[
             vmem((half, width), bf16),
+            vmem((half, head), f32),
             vmem((n_fsdp, half, depth), bf16),
             vmem((pieces, depth, head), f32),
             vmem((pieces, depth, head), f32),
@@ -536,13 +567,13 @@
             dma((n_heads,)),
         ],
         compiler_params=pltpu.CompilerParams(
-            collective_id=0, has_side_effects=True, vmem_limit_bytes=48 * 1024 * 1024
+            collective_id=0, has_side_effects=True, vmem_limit_bytes=58 * 1024 * 1024
         ),
         cost_estimate=pl.CostEstimate(
             flops=2 * n_tok * width * query_width, bytes_accessed=8 * depth * query_width,
             transcendentals=n_heads * n_tok * n_tok * n_fsdp,
         ),
-    )(shares, cos_table, sin_table, tokens, query_ckpt, key_value_ckpt)
+    )(numerators, cos_table, sin_table, tokens, query_ckpt, key_value_ckpt)
 
 
 def solution(mesh):

time: 93.1 us -> 88.8 us (0.954)
  local copies, waits for them, and re-layouts: 3.42 us -> 1.87 us
  other arithmetic: 2.65 us -> 1.39 us
    unnamed x5 -> x1, local copies, waits for them, and re-layouts: 3.42 us -> 1.87 us
    reduce_sum x1 -> x0, other arithmetic: 1.29 us -> none  [fused_local(): jnp.sum(numerators).astype(jnp.float32)]
where the time goes in v2:
time: 88.8 us; the launch traced here: 88.6 us
  Pallas kernels  85.4 us (96%)
  local copies, waits for them, and re-layouts  1.87 us (2%)
  other arithmetic  1.39 us (2%)
    pallas_call x1, Pallas kernels, fused_local(): pl.pallas_call(functools.partial(fused_kernel, n_line), out_shape=jax.Sha...  85.4 us
    unnamed x1, local copies, waits for them, and re-layouts  1.87 us

profile of v2, /device:TPU:29, one launch (start us, length us, event | category | flops | bytes accessed | tf_op | source)
XLA Modules:
  0.0 88.6 jit_solution(1593518151724194075)
XLA Ops:
  0.0 0.5 fusion
  0.6 0.8 pad_maximum_fusion
  1.4 85.4 %shard_map.46 = bf16[256,1024]{1,0:T(8,128)(2,1)} custom-call(s32[2]{0:T(128)} %num_ref.1, f32[256,128]{1,0:T(8,128)} %get-tuple-element.8.cos_ref, f32[256,128]{1,0:T(8,128)} %get-tuple-element.9.sin_ref, bf16[256,8192]{1,0:T(8,128)(2,1)} %tok_hbm.1, f32[1,512,1024]{2,1,0:T(8,128)} %query_hbm.1, f32[1,512,256]{2,1,0:T(8,128)} %pair_hbm.1), custom_call_target="tpu_custom_call" | custom-call | flops 4294967296 | bytes 4194304 | tf_op jit(solution)/shard_map/pallas_call | solution.py:523
  86.8 1.9 %copy.6 = bf16[256,1024]{1,0:T(8,128)(2,1)} copy(bf16[256,1024]{1,0:T(8,128)(2,1)} %shard_map.46) | data formatting | bytes 1048576
  (2 shorter events, 0.0 us)

commit v3 on v2

--- a/solution.py
+++ b/solution.py
@@ -115,7 +115,7 @@
 
 def fused_kernel(
     n_line, num_ref, cos_ref, sin_ref, tok_hbm, query_hbm, pair_hbm, out_ref,
-    raw, inv_rms, nrm, mine, theirs, wbuf, tok, acc, rsend, rrecv, qrot, kvb,
+    raw, inv_rms, nrm, mine, theirs, wbuf, tok, acc, rsend, rrecv, qrot, kvb, score_buf,
     raw_sem, mine_sem, ck_s, ck_r, w_s, w_r, tl_sem, tp_s, tp_r, ts_s, ts_r,
     rs_s, rs_r, kz_s, kp_s, kb_s, kz_r, ks_r, o_s, o_r,
 ):
@@ -302,10 +302,8 @@
         near(k)
     for c in range(n_line):
         tok_collect(c)
-        if c + 1 < pieces:
-            middle(c + 1)
-    for k in range(n_line + 1, pieces):
-        middle(k)
+        if c == 0:
+            middle(1)
     for c in range(n_line):
         tok_own(c).wait()
         for q in range(plane):
@@ -401,6 +399,7 @@
         for b in range(n_fsdp):
             kv_from_sib(b).wait_recv()
 
+    pair = 2
     block = 2 * n_tok
     scale = math.log2(math.e) / math.sqrt(head)
 
@@ -411,62 +410,77 @@
     def query(h):
         qrot[h] = rotate(total(h + 1)).astype(jnp.bfloat16)
 
-    def attend(h):
-        q = qrot[h]
-
-        def step(i, carry, masked):
-            top, norm, mixed = carry
-            rows = pl.ds(pl.multiple_of(i * block, block), block)
-            scores = lax.dot_general(
-                q, kvb[0, rows, :], (((1,), (1,)), ((), ())), preferred_element_type=jnp.float32
+    def attend(h0):
+        q = qrot[h0 : h0 + pair].reshape(pair * n_tok, head)
+        last = (f * n_tok) // block
+
+        def lanes(values, op):
+            groups = [values[:, g * head : (g + 1) * head] for g in range(block // head)]
+            return functools.reduce(op, groups)
+
+        def rows_of(i):
+            return pl.ds(pl.multiple_of(i * block, block), block)
+
+        def score(i):
+            return lax.dot_general(
+                q, kvb[0, rows_of(i), :], (((1,), (1,)), ((), ())),
+                preferred_element_type=jnp.float32,
             )
-            if masked:
-                row = lax.broadcasted_iota(jnp.int32, scores.shape, 0) + f * n_tok
-                col = lax.broadcasted_iota(jnp.int32, scores.shape, 1) + i * block
-                scores = jnp.where(col <= row, scores, masked_score)
-            new_top = jnp.maximum(top, jnp.max(scores, axis=1, keepdims=True))
-            weights = jnp.exp2((scores - new_top) * scale)
-            fade = jnp.exp2((top - new_top) * scale)
-            norm = norm * fade + jnp.sum(weights, axis=1, keepdims=True)
-            mixed = mixed * fade + jnp.dot(
-                weights.astype(jnp.bfloat16), kvb[1, rows, :], preferred_element_type=jnp.float32
+
+        def scored(i, top):
+            scores = score(i)
+            score_buf[i] = scores
+            return jnp.maximum(top, lanes(scores, jnp.maximum))
+
+        scores = score(last)
+        row = lax.rem(lax.broadcasted_iota(jnp.int32, scores.shape, 0), n_tok) + f * n_tok
+        col = lax.broadcasted_iota(jnp.int32, scores.shape, 1) + last * block
+        scores = jnp.where(col <= row, scores, masked_score)
+        score_buf[last] = scores
+        top = lax.fori_loop(0, last, scored, lanes(scores, jnp.maximum))
+        top = jnp.max(top, axis=1, keepdims=True)
+
+        def weighted(i, carry):
+            norm, mixed = carry
+            weights = jnp.exp2((score_buf[i] - top) * scale)
+            mixed += jnp.dot(
+                weights.astype(jnp.bfloat16), kvb[1, rows_of(i), :],
+                preferred_element_type=jnp.float32,
             )
-            return new_top, norm, mixed
-
-        last = (f * n_tok) // block
-        carry = (
-            jnp.full((n_tok, 1), masked_score, jnp.float32),
-            jnp.zeros((n_tok, 1), jnp.float32),
-            jnp.zeros((n_tok, head), jnp.float32),
-        )
-        carry = step(last, carry, True)
-        _, norm, mixed = lax.fori_loop(0, last, functools.partial(step, masked=False), carry)
-        col = pl.ds(pl.multiple_of((r * n_heads + h) * head, head), head)
-        out_ref[:, col] = (mixed / norm).astype(jnp.bfloat16)
-        out_copy(h, r).start()
+            return norm + lanes(weights, jnp.add), mixed
+
+        empty = jnp.zeros((pair * n_tok, head), jnp.float32)
+        norm, mixed = lax.fori_loop(0, last + 1, weighted, (empty, empty))
+        mixed = (mixed / jnp.sum(norm, axis=1, keepdims=True)).astype(jnp.bfloat16)
+        for i in range(pair):
+            cols = pl.ds(pl.multiple_of((r * n_heads + h0 + i) * head, head), head)
+            out_ref[:, cols] = mixed[i * n_tok : (i + 1) * n_tok, :]
+            out_copy(h0 + i, r).start()
 
     far(0)
     multiply(0)
     far(1)
     multiply(1)
     kv_begin()
+    middle(2)
+    kv_step(1, min(2, n_line))
+    middle(3)
+    kv_step(2, n_line - 1)
+    middle(4)
     far(2)
     multiply(2)
-    kv_step(1, min(2, n_line))
+    kv_step(max(2, n_line - 1), n_line)
     far(3)
     multiply(3)
-    kv_step(2, n_line)
+    query(0)
+    query(1)
+    kv_end()
     far(4)
     multiply(4)
-    query(0)
-    query(1)
+    attend(0)
     query(2)
-    kv_end()
-    attend(0)
-    attend(1)
+    query(3)
     attend(2)
-    query(3)
-    attend(3)
 
     for k in range(pieces):
         sib_ckpt(k).wait_send()
@@ -545,6 +559,7 @@
             vmem((pieces, plane, n_tok, head), bf16),
             vmem((n_heads, n_tok, head), bf16),
             vmem((2, n_fsdp * n_tok, head), bf16),
+            vmem((n_fsdp // 2, 2 * n_tok, 2 * n_tok), f32),
             dma,
             dma((pieces,)),
             dma((pieces,)),

time: 88.8 us -> 82.7 us (0.931)
  Pallas kernels: 85.4 us -> 79.2 us
    pallas_call x1, Pallas kernels: 85.4 us -> 79.2 us  [fused_local(): pl.pallas_call(functools.partial(fused_kernel, n_line), out_shape=jax.Sha...]
where the time goes in v3:
time: 82.7 us; the launch traced here: 82.5 us
  Pallas kernels  79.2 us (96%)
  local copies, waits for them, and re-layouts  1.87 us (2%)
  other arithmetic  1.39 us (2%)
    pallas_call x1, Pallas kernels, fused_local(): pl.pallas_call(functools.partial(fused_kernel, n_line), out_shape=jax.Sha...  79.2 us
    unnamed x1, local copies, waits for them, and re-layouts  1.87 us

profile of v3, /device:TPU:29, one launch (start us, length us, event | category | flops | bytes accessed | tf_op | source)
XLA Modules:
  0.0 82.5 jit_solution(13465821153443269072)
XLA Ops:
  0.0 0.5 fusion
  0.6 0.8 %pad_maximum_fusion = (f32[256,128]{1,0:T(8,128)}, f32[256,128]{1,0:T(8,128)}) fusion(f32[256,64]{1,0:T(8,128)S(1)} %get-tuple-element.7, f32[256,64]{1,0:T(8,128)S(1)} %get-tuple-element.6, f32[256,64]{1,0:T(8,128)S(1)} %get-tuple-element.5), kind=kLoop, calls=%fused_computation.2 | loop fusion | flops 65536 | bytes 458752 | tf_op jit(solution)/shard_map/concatenate | solution.py:533
  1.4 79.2 %shard_map.46 = bf16[256,1024]{1,0:T(8,128)(2,1)} custom-call(s32[2]{0:T(128)} %num_ref.1, f32[256,128]{1,0:T(8,128)} %get-tuple-element.8.cos_ref, f32[256,128]{1,0:T(8,128)} %get-tuple-element.9.sin_ref, bf16[256,8192]{1,0:T(8,128)(2,1)} %tok_hbm.1, f32[1,512,1024]{2,1,0:T(8,128)} %query_hbm.1, f32[1,512,256]{2,1,0:T(8,128)} %pair_hbm.1), custom_call_target="tpu_custom_call" | custom-call | flops 4294967296 | bytes 4194304 | tf_op jit(solution)/shard_map/pallas_call | solution.py:537
  80.6 1.9 %copy.6 = bf16[256,1024]{1,0:T(8,128)(2,1)} copy(bf16[256,1024]{1,0:T(8,128)(2,1)} %shard_map.46) | data formatting | bytes 1048576
  (2 shorter events, 0.0 us)

commit v4 on v3

--- a/solution.py
+++ b/solution.py
@@ -302,8 +302,8 @@
         near(k)
     for c in range(n_line):
         tok_collect(c)
-        if c == 0:
-            middle(1)
+        if c < 2:
+            middle(c + 1)
     for c in range(n_line):
         tok_own(c).wait()
         for q in range(plane):
@@ -399,7 +399,6 @@
         for b in range(n_fsdp):
             kv_from_sib(b).wait_recv()
 
-    pair = 2
     block = 2 * n_tok
     scale = math.log2(math.e) / math.sqrt(head)
 
@@ -410,8 +409,9 @@
     def query(h):
         qrot[h] = rotate(total(h + 1)).astype(jnp.bfloat16)
 
-    def attend(h0):
-        q = qrot[h0 : h0 + pair].reshape(pair * n_tok, head)
+    def attend(h0, count):
+        n_rows = count * n_tok
+        q = qrot[h0 : h0 + count].reshape(n_rows, head)
         last = (f * n_tok) // block
 
         def lanes(values, op):
@@ -429,30 +429,30 @@
 
         def scored(i, top):
             scores = score(i)
-            score_buf[i] = scores
+            score_buf[i, :n_rows, :] = scores
             return jnp.maximum(top, lanes(scores, jnp.maximum))
 
         scores = score(last)
         row = lax.rem(lax.broadcasted_iota(jnp.int32, scores.shape, 0), n_tok) + f * n_tok
         col = lax.broadcasted_iota(jnp.int32, scores.shape, 1) + last * block
         scores = jnp.where(col <= row, scores, masked_score)
-        score_buf[last] = scores
+        score_buf[last, :n_rows, :] = scores
         top = lax.fori_loop(0, last, scored, lanes(scores, jnp.maximum))
         top = jnp.max(top, axis=1, keepdims=True)
 
         def weighted(i, carry):
             norm, mixed = carry
-            weights = jnp.exp2((score_buf[i] - top) * scale)
+            weights = jnp.exp2((score_buf[i, :n_rows, :] - top) * scale)
             mixed += jnp.dot(
                 weights.astype(jnp.bfloat16), kvb[1, rows_of(i), :],
                 preferred_element_type=jnp.float32,
             )
             return norm + lanes(weights, jnp.add), mixed
 
-        empty = jnp.zeros((pair * n_tok, head), jnp.float32)
+        empty = jnp.zeros((n_rows, head), jnp.float32)
         norm, mixed = lax.fori_loop(0, last + 1, weighted, (empty, empty))
         mixed = (mixed / jnp.sum(norm, axis=1, keepdims=True)).astype(jnp.bfloat16)
-        for i in range(pair):
+        for i in range(count):
             cols = pl.ds(pl.multiple_of((r * n_heads + h0 + i) * head, head), head)
             out_ref[:, cols] = mixed[i * n_tok : (i + 1) * n_tok, :]
             out_copy(h0 + i, r).start()
@@ -462,7 +462,6 @@
     far(1)
     multiply(1)
     kv_begin()
-    middle(2)
     kv_step(1, min(2, n_line))
     middle(3)
     kv_step(2, n_line - 1)
@@ -475,12 +474,13 @@
     query(0)
     query(1)
     kv_end()
+    attend(0, 2)
     far(4)
     multiply(4)
-    attend(0)
     query(2)
+    attend(2, 1)
     query(3)
-    attend(2)
+    attend(3, 1)
 
     for k in range(pieces):
         sib_ckpt(k).wait_send()

time: 82.7 us -> 85.9 us (1.039)
  Pallas kernels: 79.2 us -> 82.4 us
    pallas_call x1, Pallas kernels: 79.2 us -> 82.4 us  [fused_local(): pl.pallas_call(functools.partial(fused_kernel, n_line), out_shape=jax.Sha...]
where the time goes in v4:
time: 85.9 us; the launch traced here: 85.7 us
  Pallas kernels  82.4 us (96%)
  local copies, waits for them, and re-layouts  1.87 us (2%)
  other arithmetic  1.39 us (2%)
    pallas_call x1, Pallas kernels, fused_local(): pl.pallas_call(functools.partial(fused_kernel, n_line), out_shape=jax.Sha...  82.4 us
    unnamed x1, local copies, waits for them, and re-layouts  1.87 us

profile of v4, /device:TPU:29, one launch (start us, length us, event | category | flops | bytes accessed | tf_op | source)
XLA Modules:
  0.0 85.7 jit_solution(3804481412700183596)
XLA Ops:
  0.0 0.5 fusion
  0.6 0.8 pad_maximum_fusion
  1.4 82.4 %shard_map.46 = bf16[256,1024]{1,0:T(8,128)(2,1)} custom-call(s32[2]{0:T(128)} %num_ref.1, f32[256,128]{1,0:T(8,128)} %get-tuple-element.8.cos_ref, f32[256,128]{1,0:T(8,128)} %get-tuple-element.9.sin_ref, bf16[256,8192]{1,0:T(8,128)(2,1)} %tok_hbm.1, f32[1,512,1024]{2,1,0:T(8,128)} %query_hbm.1, f32[1,512,256]{2,1,0:T(8,128)} %pair_hbm.1), custom_call_target="tpu_custom_call" | custom-call | flops 4294967296 | bytes 4194304 | tf_op jit(solution)/shard_map/pallas_call | solution.py:537
  83.8 1.9 %copy.6 = bf16[256,1024]{1,0:T(8,128)(2,1)} copy(bf16[256,1024]{1,0:T(8,128)(2,1)} %shard_map.46) | data formatting | bytes 1048576
  (2 shorter events, 0.0 us)
